TPU v7x, 128 devices: a whole 4x4x4 slice. The times are simulated.
128 devices in a mesh: lat: 8 (over y, core), lon: 16 (over x, z).
Axes of the slice: x: 4, y: 4, z: 4, core: 2. Of those that a mesh axis runs over, the one named last changes fastest.
Arguments:
- probes: bfloat16 [8, 8, 512, 4096], P(None, None, 'lat', 'lon'), may hold values from -12 to 12
- kappa_sq: float32 [8, 512, 4096], P(None, 'lat', 'lon'), may hold values from 0.2 to 1
- cond_lat: float32 [512, 4096], P('lat', 'lon'), may hold values from 0.05 to 0.5
- cond_lon: float32 [512, 4096], P('lat', 'lon'), may hold values from 0.05 to 0.5
- innovations: float32 [8, 1048576], P(None, ('lat', 'lon')), may hold values from -6 to 6
- obs_weight: float32 [1048576], P(('lat', 'lon')), may hold values from 0.25 to 4
- station_dest: int32 [1048576, 1], P(('lat', 'lon')), may hold values from 0 to 127; in each aligned block of 8192 rows (0 to 8191, 8192 to 16383, ...) at most 128 rows name the same one
- station_cell: int32 [1048576], P(('lat', 'lon')), may hold values from 0 to 16383
Outputs:
- solution: float32 [9, 8, 512, 4096], P(None, None, 'lat', 'lon')
Inputs may be any that keep to these rules, and one draw needn't show every extreme that they name: `station_dest`: among the stations of one device, at most 128 share a destination. `station_cell`: cells are numbered row by row within the destination's block of 64 x 256.
All inputs are finite; a program needn't handle non-finite values.
Results may differ from a plain program's by a relative error of at most 0.0003.
Values sent between devices are 32-bit elements; how exact they have to be, the bound alone decides.
A program may use at most 128 MiB of HBM per device.

v0:
```python
import math

import jax
import jax.numpy as jnp
from jax import lax
from jax.sharding import PartitionSpec as P

ITERS = 2


def padded_2(block, sides, width):
    for axis, dim in sides:
        count = lax.axis_size(axis)
        forward = [(i, i + 1) for i in range(count - 1)]
        forward.append((count - 1, 0))
        backward = [(target, source) for source, target in forward]
        low = lax.ppermute(
            lax.slice_in_dim(block, block.shape[dim] - width, None, axis=dim), axis, forward
        )
        high = lax.ppermute(lax.slice_in_dim(block, 0, width, axis=dim), axis, backward)
        block = jnp.concatenate([low, block, high], axis=dim)
    return block


def extend(field):
    return padded_2(field, (("lat", 2), ("lon", 3)), 1)


def local_sum(field):
    return jnp.sum(field, axis=(2, 3))


def spread(values):
    return values[:, :, None, None]


def norm_total(resid):
    return lax.psum(local_sum(resid * resid), ("lat", "lon"))


def stencil(diag, north, south, west, east, center, upper, lower, left, right):
    return diag * center - north * upper - south * lower - west * left - east * right


def local(
    probes, kappa_sq, cond_lat, cond_lon, innovations, obs_weight, station_dest, station_cell
):
    lat_count = lax.axis_size("lat")
    lon_count = lax.axis_size("lon")
    devices = lat_count * lon_count
    levels, rows, cols = kappa_sq.shape
    held = obs_weight.shape[0]
    slots = 2 * held // devices
    highest = lax.Precision.HIGHEST
    dest = station_dest[:, 0]
    matches = (dest[:, None] == jnp.arange(devices, dtype=jnp.int32)[None, :]).astype(jnp.float32)
    block = math.gcd(held, 512)
    nblocks = held // block
    blocked = matches.reshape(nblocks, block, devices)
    lower_tri = (
        jnp.arange(block, dtype=jnp.int32)[:, None] > jnp.arange(block, dtype=jnp.int32)[None, :]
    ).astype(jnp.bfloat16)
    within = jnp.einsum(
        "ij,bjd->bid", lower_tri, blocked.astype(jnp.bfloat16), preferred_element_type=jnp.float32
    )
    block_totals = jnp.sum(blocked, axis=1)
    offsets = jnp.cumsum(block_totals, axis=0) - block_totals
    ranking = (within + offsets[:, None, :]).reshape(held, devices)
    position = jnp.sum(ranking * matches, axis=1)
    slot_hot = (position[:, None] == jnp.arange(slots, dtype=jnp.float32)[None, :]).astype(
        jnp.float32
    )
    weighted = innovations * obs_weight[None, :]
    carried = jnp.concatenate([weighted, station_cell.astype(jnp.float32)[None]], 0)
    by_dest = (carried.T[:, :, None] * matches[:, None, :]).reshape(held, (levels + 1) * devices)
    packed = jnp.einsum("sk,sq->kq", by_dest, slot_hot, precision=highest).reshape(
        levels + 1, devices, slots
    )
    outgoing = jnp.transpose(packed[:levels], (1, 0, 2))
    cell_slots = packed[levels].astype(jnp.int32)
    got_values, got_cells = (
        lax.all_to_all(
            outgoing.reshape(devices, levels * slots),
            ("lat", "lon"),
            split_axis=0,
            concat_axis=0,
            tiled=True,
        ),
        lax.all_to_all(cell_slots, ("lat", "lon"), split_axis=0, concat_axis=0, tiled=True),
    )
    got_values = got_values.reshape(devices, levels, slots)
    row_hot = (
        (got_cells // cols)[:, :, None] == jnp.arange(rows, dtype=jnp.int32)[None, None, :]
    ).astype(jnp.float32)
    col_hot = (
        (got_cells % cols)[:, :, None] == jnp.arange(cols, dtype=jnp.int32)[None, None, :]
    ).astype(jnp.float32)
    placed = got_values[:, :, :, None] * row_hot[:, None, :, :]
    adjoint = jnp.einsum("dlqr,dqc->lrc", placed, col_hot, precision=highest)
    rhs = jnp.concatenate([probes.astype(jnp.float32), adjoint[None]], 0)
    row_glob = lax.axis_index("lat") * rows + jnp.arange(rows, dtype=jnp.int32)
    south = jnp.where(row_glob[:, None] < rows * lat_count - 1, cond_lat, jnp.zeros_like(cond_lat))
    padded = extend(jnp.stack([south, cond_lon])[None])
    north = padded[0, 0, :-2, 1:-1]
    west = padded[0, 1, 1:-1, :-2]
    diag = kappa_sq + north + south + west + cond_lon

    def apply_k(field):
        wide = extend(field)
        return stencil(
            diag,
            north,
            south,
            west,
            cond_lon,
            field,
            wide[:, :, :-2, 1:-1],
            wide[:, :, 2:, 1:-1],
            wide[:, :, 1:-1, :-2],
            wide[:, :, 1:-1, 2:],
        )

    estimate = jnp.zeros_like(rhs)
    resid = rhs
    direction = rhs
    norm_now = norm_total(resid)
    for step in range(ITERS):
        once = apply_k(direction)
        image = apply_k(once)
        alpha = norm_now / lax.psum(local_sum(once * once), ("lat", "lon"))
        estimate = estimate + spread(alpha) * direction
        resid = resid - spread(alpha) * image
        if step + 1 < ITERS:
            norm_next = norm_total(resid)
            direction = resid + spread(norm_next / norm_now) * direction
            norm_now = norm_next
    return estimate


def solution(mesh):
    placed = (
        P(None, None, "lat", "lon"),
        P(None, "lat", "lon"),
        P("lat", "lon"),
        P("lat", "lon"),
        P(None, ("lat", "lon")),
        P(("lat", "lon")),
        P(("lat", "lon"), None),
        P(("lat", "lon")),
    )
    return jax.shard_map(
        local, mesh=mesh, in_specs=placed, out_specs=P(None, None, "lat", "lon"), check_vma=False
    )
```

profile of v0, /device:TPU:1, one launch (start us, length us, event | category | flops | bytes accessed | tf_op | source)
XLA Modules:
  0.0 449.5 jit_solution(14447020864038265194)
XLA Ops:
  4.9 12.8 %broadcast_multiply_fusion = f32[8192,9,128]{0,2,1:T(8,128)} fusion(f32[8192,128]{0,1:T(8,128)S(1)} %fusion.36, f32[8192,9]{0,1:T(8,128)S(1)} %maximum_bitcast_fusion), kind=kLoop, calls=%fused_computation.2 | loop fusion | flops 9437184 | bytes 42237952 | tf_op jit(solution)/shard_map/mul | solution.py:75
  17.7 21.8 %fusion.37 = f32[1152,128]{1,0:T(8,128)S(1)} fusion(f32[8192,1152]{0,1:T(8,128)} %bitcast.49, f32[8192]{0:T(1024)S(1)} %bitcast.57), kind=kOutput, calls=%fused_computation.86 | convolution fusion | flops 14496563200 | bytes 38371328 | tf_op jit(solution)/shard_map/sk,sq->kq/dot_general | solution.py:76
  40.1 11.5 %all-to-all-start.1 = ((s32[128,1,128]{2,1,0:T(1,128)}), s32[128,1,128]{2,1,0:T(1,128)S(1)}, u32[]{:S(2)}, u32[]{:S(2)}) async-start(s32[128,1,128]{2,1,0:T(1,128)} %bitcast.11), calls=%async_computation.1 | async-start | bytes 131072 | tf_op jit(solution)/shard_map/all_to_all | solution.py:89
  53.4 3.3 copy_convert_fusion
  61.0 8.9 %all-to-all-start = ((f32[128,1,1024]{2,1,0:T(1,128)}), f32[128,1,1024]{2,1,0:T(1,128)S(1)}, u32[]{:S(2)}, u32[]{:S(2)}) async-start(f32[128,1,1024]{2,1,0:T(1,128)} %copy.14), calls=%async_computation | async-start | bytes 1048576 | tf_op jit(solution)/shard_map/all_to_all | solution.py:82
  70.1 2.7 fusion.38
  72.7 10.6 %all-to-all-done = f32[128,1,1024]{2,1,0:T(1,128)S(1)} async-done(((f32[128,1,1024]{2,1,0:T(1,128)}), f32[128,1,1024]{2,1,0:T(1,128)S(1)}, u32[]{:S(2)}, u32[]{:S(2)}) %all-to-all-start) | async-done | bytes 524320 | tf_op jit(solution)/shard_map/all_to_all | solution.py:82
  83.4 12.9 %fusion.70 = f32[128,8,128,64]{2,3,0,1:T(8,128)} fusion(f32[128,128,64]{1,2,0:T(8,128)} %fusion.38, f32[128,8,128]{2,0,1:T(8,128)S(1)} %copy.16), kind=kLoop, calls=%fused_computation.1.clone.clone.clone.2 | loop fusion | flops 8388608 | bytes 38273024 | tf_op jit(solution)/shard_map/dlqr,dqc->lrc/dot_general | solution.py:99
  96.3 22.4 %fusion.41 = f32[1,8,64,256]{3,2,1,0:T(8,128)S(1)} fusion(s32[128,128]{1,0:T(8,128)S(1)} %get-tuple-element.28, f32[128,8,128,64]{2,3,0,1:T(8,128)} %fusion.70), kind=kOutput, calls=%fused_computation.91 | convolution fusion | flops 25773998080 | bytes 34144256 | tf_op jit(solution)/shard_map/dlqr,dqc->lrc/dot_general | solution.py:99
  121.9 2.7 collective-permute-done.4
  127.4 3.2 copy.20
  132.8 4.7 %collective-permute-start.6 = (f32[9,8,66,1]{2,1,3,0:T(8,128)}, f32[9,8,66,1]{2,1,3,0:T(8,128)}, u32[]{:S(2)}, u32[]{:S(2)}) collective-permute-start(f32[9,8,66,1]{2,1,3,0:T(8,128)} %copy.22), channel_id=1, source_target_pairs={{1,0},{2,1},{3,2},{4,3},{5,4},{6,5},{7,6},{8,7},{9,8},{10,9},{11,1... | collective-permute-start | bytes 57032 | tf_op jit(solution)/shard_map/ppermute | solution.py:20
  140.7 3.1 copy.23
  143.8 14.0 %multiply_reduce_fusion.1 = (f32[9,8]{1,0:T(8,128)S(1)}, f32[9,8,64,256]{3,1,2,0:T(8,128)S(1)}) fusion(f32[9,8,66,1]{3,1,2,0:T(8,128)} %copy.23, f32[9,8,1,256]{3,1,2,0:T(8,128)} %copy-done.8, f32[1,8,64,256]{3,1,2,0:T(8,128)S(1)} %copy.18, f32[8,8,64,256]{3,1,2,0:T(8,128)} %copy_convert_fusion, f32[9,8,1,256]{3,1,2,0:T(8,128)} %copy-done.7, ...), kind=kLoop, calls=%fused_computation.75 | loop fusion | flops 28311480 | bytes 10409376 | tf_op jit(solution)/shard_map/reduce_sum | solution.py:30
  163.1 2.2 fusion.57
  165.4 3.2 copy.24
  170.1 4.8 %collective-permute-start.10 = (f32[9,8,66,1]{2,1,3,0:T(8,128)}, f32[9,8,66,1]{2,1,3,0:T(8,128)}, u32[]{:S(2)}, u32[]{:S(2)}) collective-permute-start(f32[9,8,66,1]{2,1,3,0:T(8,128)} %copy.26), channel_id=1, source_target_pairs={{1,0},{2,1},{3,2},{4,3},{5,4},{6,5},{7,6},{8,7},{9,8},{10,9},{11,1... | collective-permute-start | bytes 57032 | tf_op jit(solution)/shard_map/ppermute | solution.py:20
  174.9 2.6 multiply_reduce_fusion.2
  177.5 66.7 %all-reduce = (f32[9,8]{1,0:T(8,128)S(1)}, f32[9,8]{1,0:T(8,128)S(1)}) all-reduce(f32[9,8]{1,0:T(8,128)S(1)} %multiply_reduce_fusion.2, f32[9,8]{1,0:T(8,128)S(1)} %get-tuple-element.9), channel_id=1, replica_groups=mesh['lat'=8,'lon'=16] {'lat','lon'}, use_global_device_ids=true, to_apply=%region_4.5 | all-reduce | flops 144 | bytes 1152 | tf_op jit(solution)/shard_map/psum | solution.py:38
  246.5 3.1 copy.27
  249.7 17.6 %multiply_reduce_fusion = (f32[9,8]{1,0:T(8,128)}, f32[9,8,64,256]{3,1,2,0:T(8,128)}) fusion(f32[9,8,66,1]{3,1,2,0:T(8,128)} %copy.27, f32[9,8,1,256]{3,1,2,0:T(8,128)} %copy-done.10, f32[9,8,64,256]{3,1,2,0:T(8,128)} %copy-done.2, f32[9,8,1,256]{3,1,2,0:T(8,128)} %copy-done.9, f32[64,256]{1,0:T(8,128)} %param.11, f32[9,8,66,1]{3,1,2,0:T(8,128)S(1)} %copy.25, ...), kind=kLoop, calls=%fused_computation.74 | loop fusion | flops 25952184 | bytes 15128256 | tf_op jit(solution)/shard_map/reduce_sum | solution.py:30
  267.3 62.5 %psum.30 = f32[9,8]{1,0:T(8,128)S(1)} all-reduce(f32[9,8]{1,0:T(8,128)} %get-tuple-element.7), channel_id=1, replica_groups=mesh['lat'=8,'lon'=16] {'lat','lon'}, use_global_device_ids=true, to_apply=%region_8.9 | all-reduce | flops 72 | bytes 576 | tf_op jit(solution)/shard_map/psum | solution.py:38
  330.5 4.3 multiply_add_fusion.1
  338.1 2.4 collective-permute-done.12
  341.5 2.2 fusion.56
  343.8 3.2 copy.28
  348.5 5.0 %collective-permute-start.14 = (f32[9,8,66,1]{2,1,3,0:T(8,128)}, f32[9,8,66,1]{2,1,3,0:T(8,128)}, u32[]{:S(2)}, u32[]{:S(2)}) collective-permute-start(f32[9,8,66,1]{2,1,3,0:T(8,128)} %copy.30), channel_id=1, source_target_pairs={{1,0},{2,1},{3,2},{4,3},{5,4},{6,5},{7,6},{8,7},{9,8},{10,9},{11,1... | collective-permute-start | bytes 57032 | tf_op jit(solution)/shard_map/ppermute | solution.py:20
  355.3 3.2 copy.31
  358.4 15.4 %fusion.10 = f32[9,8]{1,0:T(8,128)} fusion(f32[9,8,66,1]{3,1,2,0:T(8,128)} %copy.31, f32[9,8,1,256]{3,1,2,0:T(8,128)} %copy-done.12, f32[9,8,64,256]{3,1,2,0:T(8,128)} %copy-done.1, f32[9,8,1,256]{3,1,2,0:T(8,128)} %copy-done.11, f32[9,8,66,1]{3,1,2,0:T(8,128)S(1)} %copy.29, f32[64,256]{1,0:T(8,128)} %param.11, f32[64,256]{1,0:T(8,128)} %copy-done.6, ...), kind=kLoop, calls=%fused_computation.20 | loop fusion | flops 22413240 | bytes 5690784 | tf_op jit(solution)/shard_map/reduce_sum | solution.py:30
  373.8 66.8 %psum.31 = f32[9,8]{1,0:T(8,128)S(1)} all-reduce(f32[9,8]{1,0:T(8,128)} %fusion.10), channel_id=1, replica_groups=mesh['lat'=8,'lon'=16] {'lat','lon'}, use_global_device_ids=true, to_apply=%region_10.11 | all-reduce | flops 72 | bytes 576 | tf_op jit(solution)/shard_map/psum | solution.py:130
  441.4 4.3 multiply_add_fusion
  445.7 3.6 copy.32
  (110 shorter events, 41.2 us)
Async XLA Ops:
  2.5 2.2 copy-start.19
  2.6 2.2 copy-start.13
  2.6 2.2 copy-start.17
  17.7 33.9 %copy-start.14 = (f32[64,256]{1,0:T(8,128)S(1)}, f32[64,256]{1,0:T(8,128)}, u32[]{:S(2)}) copy-start(f32[64,256]{1,0:T(8,128)} %param.10) | copy-start | bytes 196612
  17.7 34.0 %copy-start.4 = (f32[64,256]{1,0:T(8,128)S(1)}, f32[64,256]{1,0:T(8,128)}, u32[]{:S(2)}) copy-start(f32[64,256]{1,0:T(8,128)} %param.11) | copy-start | bytes 196612
  17.7 35.7 %copy-start.3 = (bf16[8,8,64,256]{3,2,1,0:T(8,128)(2,1)S(1)}, bf16[8,8,64,256]{3,2,1,0:T(8,128)(2,1)}, u32[]{:S(2)}) copy-start(bf16[8,8,64,256]{3,2,1,0:T(8,128)(2,1)} %param.8) | copy-start | bytes 6291460
  40.1 21.0 %all-to-all-start.1 = ((s32[128,1,128]{2,1,0:T(1,128)}), s32[128,1,128]{2,1,0:T(1,128)S(1)}, u32[]{:S(2)}, u32[]{:S(2)}) async-start(s32[128,1,128]{2,1,0:T(1,128)} %bitcast.11), calls=%async_computation.1 | async-start | bytes 131072 | tf_op jit(solution)/shard_map/all_to_all | solution.py:89
  51.7 6.4 %collective-permute-start = (f32[1,2,1,256]{3,2,1,0:T(1,128)S(1)}, f32[1,2,1,256]{3,2,1,0:T(1,128)S(1)}, u32[]{:S(2)}, u32[]{:S(2)}) collective-permute-start(f32[1,2,1,256]{3,2,1,0:T(1,128)S(1)} %get-tuple-element.25), channel_id=1, source_target_pairs={{0,16},{16,32},{32,48},{48,64},{64,80},{80,96},{96,112},{112,0},{1... | collective-permute-start | bytes 6152 | tf_op jit(solution)/shard_map/ppermute | solution.py:17
  53.4 4.7 %collective-permute-start.1 = (f32[1,2,1,256]{3,2,1,0:T(1,128)S(1)}, f32[1,2,1,256]{3,2,1,0:T(1,128)S(1)}, u32[]{:S(2)}, u32[]{:S(2)}) collective-permute-start(f32[1,2,1,256]{3,2,1,0:T(1,128)S(1)} %get-tuple-element.26), channel_id=1, source_target_pairs={{16,0},{32,16},{48,32},{64,48},{80,64},{96,80},{112,96},{0,112},{1... | collective-permute-start | bytes 6152 | tf_op jit(solution)/shard_map/ppermute | solution.py:20
  58.2 62.3 %collective-permute-start.2 = (f32[1,2,66,1]{3,2,1,0:T(8,128)S(1)}, f32[1,2,66,1]{3,2,1,0:T(8,128)S(1)}, u32[]{:S(2)}, u32[]{:S(2)}) collective-permute-start(f32[1,2,66,1]{3,2,1,0:T(8,128)S(1)} %pad_maximum_fusion.32), channel_id=1, source_target_pairs={{0,1},{1,2},{2,3},{3,4},{4,5},{5,6},{6,7},{7,8},{8,9},{9,10},{10,1... | collective-permute-start | bytes 1592 | tf_op jit(solution)/shard_map/ppermute | solution.py:17
  61.0 22.2 %all-to-all-start = ((f32[128,1,1024]{2,1,0:T(1,128)}), f32[128,1,1024]{2,1,0:T(1,128)S(1)}, u32[]{:S(2)}, u32[]{:S(2)}) async-start(f32[128,1,1024]{2,1,0:T(1,128)} %copy.14), calls=%async_computation | async-start | bytes 1048576 | tf_op jit(solution)/shard_map/all_to_all | solution.py:82
  96.3 22.7 %copy-start = (f32[8,8,64,256]{3,1,2,0:T(8,128)S(1)}, f32[8,8,64,256]{3,1,2,0:T(8,128)}, u32[]{:S(2)}) copy-start(f32[8,8,64,256]{3,1,2,0:T(8,128)} %copy_convert_fusion) | copy-start | bytes 12582916
  119.0 2.9 collective-permute-start.3
  120.5 4.1 collective-permute-start.4
  120.6 16.9 %copy-start.5 = (f32[64,256]{1,0:T(8,128)}, f32[64,256]{1,0:T(8,128)S(1)}, u32[]{:S(2)}) copy-start(f32[64,256]{1,0:T(8,128)S(1)} %get-tuple-element.23) | copy-start | bytes 196612
  120.6 16.9 %copy-start.6 = (f32[64,256]{1,0:T(8,128)}, f32[64,256]{1,0:T(8,128)S(1)}, u32[]{:S(2)}) copy-start(f32[64,256]{1,0:T(8,128)S(1)} %get-tuple-element.24) | copy-start | bytes 196612
  121.9 2.7 copy-start.7
  130.6 8.3 %collective-permute-start.5 = (f32[9,8,66,1]{2,1,3,0:T(8,128)}, f32[9,8,66,1]{2,1,3,0:T(8,128)}, u32[]{:S(2)}, u32[]{:S(2)}) collective-permute-start(f32[9,8,66,1]{2,1,3,0:T(8,128)} %copy.20), channel_id=1, source_target_pairs={{0,1},{1,2},{2,3},{3,4},{4,5},{5,6},{6,7},{7,8},{8,9},{9,10},{10,1... | collective-permute-start | bytes 57032 | tf_op jit(solution)/shard_map/ppermute | solution.py:17
  132.8 7.9 %collective-permute-start.6 = (f32[9,8,66,1]{2,1,3,0:T(8,128)}, f32[9,8,66,1]{2,1,3,0:T(8,128)}, u32[]{:S(2)}, u32[]{:S(2)}) collective-permute-start(f32[9,8,66,1]{2,1,3,0:T(8,128)} %copy.22), channel_id=1, source_target_pairs={{1,0},{2,1},{3,2},{4,3},{5,4},{6,5},{7,6},{8,7},{9,8},{10,9},{11,1... | collective-permute-start | bytes 57032 | tf_op jit(solution)/shard_map/ppermute | solution.py:20
  157.8 5.2 %copy-start.2 = (f32[9,8,64,256]{3,1,2,0:T(8,128)}, f32[9,8,64,256]{3,1,2,0:T(8,128)S(1)}, u32[]{:S(2)}) copy-start(f32[9,8,64,256]{3,1,2,0:T(8,128)S(1)} %get-tuple-element.10) | copy-start | bytes 14155780
  157.8 2.6 collective-permute-start.7
  158.7 3.8 collective-permute-start.8
  160.5 2.5 copy-start.9
  168.6 76.2 %collective-permute-start.9 = (f32[9,8,66,1]{2,1,3,0:T(8,128)}, f32[9,8,66,1]{2,1,3,0:T(8,128)}, u32[]{:S(2)}, u32[]{:S(2)}) collective-permute-start(f32[9,8,66,1]{2,1,3,0:T(8,128)} %copy.24), channel_id=1, source_target_pairs={{0,1},{1,2},{2,3},{3,4},{4,5},{5,6},{6,7},{7,8},{8,9},{9,10},{10,1... | collective-permute-start | bytes 57032 | tf_op jit(solution)/shard_map/ppermute | solution.py:17
  170.1 76.4 %collective-permute-start.10 = (f32[9,8,66,1]{2,1,3,0:T(8,128)}, f32[9,8,66,1]{2,1,3,0:T(8,128)}, u32[]{:S(2)}, u32[]{:S(2)}) collective-permute-start(f32[9,8,66,1]{2,1,3,0:T(8,128)} %copy.26), channel_id=1, source_target_pairs={{1,0},{2,1},{3,2},{4,3},{5,4},{6,5},{7,6},{8,7},{9,8},{10,9},{11,1... | collective-permute-start | bytes 57032 | tf_op jit(solution)/shard_map/ppermute | solution.py:20
  329.8 5.0 %copy-start.16 = (f32[9,8]{1,0:T(8,128)}, f32[9,8]{1,0:T(8,128)S(1)}, u32[]{:S(2)}) copy-start(f32[9,8]{1,0:T(8,128)S(1)} %psum.30) | copy-start | bytes 868
  334.8 6.7 %copy-start.1 = (f32[9,8,64,256]{3,1,2,0:T(8,128)}, f32[9,8,64,256]{3,1,2,0:T(8,128)S(1)}, u32[]{:S(2)}) copy-start(f32[9,8,64,256]{3,1,2,0:T(8,128)S(1)} %multiply_add_fusion.1) | copy-start | bytes 14155780
  334.9 3.2 collective-permute-start.11
  336.7 3.8 collective-permute-start.12
  338.1 2.4 copy-start.11
  347.0 6.5 %collective-permute-start.13 = (f32[9,8,66,1]{2,1,3,0:T(8,128)}, f32[9,8,66,1]{2,1,3,0:T(8,128)}, u32[]{:S(2)}, u32[]{:S(2)}) collective-permute-start(f32[9,8,66,1]{2,1,3,0:T(8,128)} %copy.28), channel_id=1, source_target_pairs={{0,1},{1,2},{2,3},{3,4},{4,5},{5,6},{6,7},{7,8},{8,9},{9,10},{10,1... | collective-permute-start | bytes 57032 | tf_op jit(solution)/shard_map/ppermute | solution.py:17
  348.5 6.7 %collective-permute-start.14 = (f32[9,8,66,1]{2,1,3,0:T(8,128)}, f32[9,8,66,1]{2,1,3,0:T(8,128)}, u32[]{:S(2)}, u32[]{:S(2)}) collective-permute-start(f32[9,8,66,1]{2,1,3,0:T(8,128)} %copy.30), channel_id=1, source_target_pairs={{1,0},{2,1},{3,2},{4,3},{5,4},{6,5},{7,6},{8,7},{9,8},{10,9},{11,1... | collective-permute-start | bytes 57032 | tf_op jit(solution)/shard_map/ppermute | solution.py:20
  (5 other events, 4.3 us)
where the time goes:
time: 459 us; the launch traced here: 450 us
  blocking collectives  196 us (43%)
  other arithmetic  97.4 us (21%)
  matrix products  45.8 us (10%)
  starting transfers between devices  43.8 us (10%)
  local copies, waits for them, and re-layouts  43.3 us (9%)
  waiting for transfers between devices  22.5 us (5%)
    psum x2, blocking collectives, norm_total(): return lax.psum(local_sum(resid * resid), ('lat', 'lon'))  129 us
    psum x1, blocking collectives, local(): alpha = norm_now / lax.psum(local_sum(once * once), ('lat', 'lon'))  66.8 us
    reduce_sum x4, other arithmetic, local_sum(): return jnp.sum(field, axis=(2, 3))  49.7 us
    dot_general x1, matrix products, local(): adjoint = jnp.einsum('dlqr,dqc->lrc', placed, col_hot, precision=highest)  22.4 us
    dot_general x1, matrix products, local(): jnp.einsum('sk,sq->kq', by_dest, slot_hot, precision=highest)  21.8 us
    slice x9, local copies, waits for them, and re-layouts, padded_2(): lax.slice_in_dim(block, block.shape[dim] - width, None, axis=dim)  16.3 us
    ppermute x7, starting transfers between devices, padded_2(): lax.ppermute(lax.slice_in_dim(block, 0, width, axis=dim), axis, backward)  15.5 us
    dot_general x1, other arithmetic, local(): adjoint = jnp.einsum('dlqr,dqc->lrc', placed, col_hot, precision=highest)  12.9 us
  transfers between devices with their start and end apart: 17, of which 8 were waited for; matrix products, arithmetic and copies ran while one was open for 13% of the time, Pallas kernels for 0%

commit v1 on v0

v1 whole, which is shorter than its diff:
```python
import functools

import jax
import jax.numpy as jnp
from jax import lax
from jax.experimental import pallas as pl
from jax.experimental.pallas import tpu as pltpu
from jax.sharding import PartitionSpec as P

f32, bf16, i32 = jnp.float32, jnp.bfloat16, jnp.int32
MESH = pl.DeviceIdType.MESH
LAT, LON, DEV = 8, 16, 128
LEVELS, ROWS, COLS = 8, 64, 256
NP, NA, NF = 64, 8, 72
PAD = ROWS + 16
HELD, SLOTS = 8192, 128
NT = (((1,), (1,)), ((), ()))
STEP_MIN, STEP_MAX = 1.0 / 25.0, 1.0 / 0.04


def iota(shape, dim):
    return lax.broadcasted_iota(i32, shape, dim)


def split2(v):
    hi = v.astype(bf16)
    return hi, (v - hi.astype(f32)).astype(bf16)


def one_hot(mask):
    return jnp.where(mask, 1.0, 0.0).astype(bf16)


def flat_rows(block, count):
    return jnp.concatenate([block[i : i + 1] for i in range(count)], 1)


def rank_phase(dest, pos, carry, span=256):
    upper = one_hot(iota((span, span), 0) < iota((span, span), 1))
    carry[...] = jnp.zeros((DEV, 128), f32)

    def body(c, _):
        s0 = pl.multiple_of(c * span, span)
        mask = iota((DEV, span), 0) == dest[:, pl.ds(s0, span)]
        hot = jnp.where(mask, 1.0, 0.0)
        within = jnp.dot(hot.astype(bf16), upper, preferred_element_type=f32)
        before = jnp.concatenate([carry[...]] * (span // 128), 1)
        pos[:, pl.ds(s0, span)] = jnp.sum(jnp.where(mask, within + before, 0.0), axis=0, keepdims=True)
        carry[...] += jnp.sum(hot, axis=1, keepdims=True)
        return 0

    lax.fori_loop(0, HELD // span, body, 0, unroll=4)


def pack_phase(inno, weight, dest, cell, pos, acc, send, span=1024):
    acc[...] = jnp.zeros((576, 256), f32)
    part = span // 128

    def body(c, _):
        s0 = pl.multiple_of(c * span, span)
        r0 = pl.multiple_of(c * part, part)
        d = dest[:, pl.ds(s0, span)]
        d_hi = jnp.where(d >= 64, 1, 0)
        d_lo = d - d_hi * 64
        slot = pos[:, pl.ds(s0, span)].astype(i32) + d_hi * SLOTS
        hi, lo = split2(inno[:, pl.ds(s0, span)] * flat_rows(weight[pl.ds(r0, part), :], part))
        cells = flat_rows(cell[pl.ds(r0, part), :], part)
        c_row = cells // COLS
        cell_hi = (c_row * COLS).astype(f32).astype(bf16)
        cell_lo = (cells - c_row * COLS).astype(f32).astype(bf16)
        slot_hot = one_hot(iota((256, span), 0) == slot)
        hi2, lo2 = jnp.concatenate([hi, hi], 0), jnp.concatenate([lo, lo], 0)
        pair = iota((16, span), 0) // 8
        left_hi, left_lo = [], []
        for t in range(32):
            mine = one_hot((pair + 2 * t) == d_lo)
            left_hi.append(mine * hi2)
            left_lo.append(mine * lo2)
        mine = one_hot(iota((64, span), 0) == d_lo)
        left_hi.append(mine * cell_hi)
        left_lo.append(mine * cell_lo)
        acc[...] += lax.dot_general(
            jnp.concatenate(left_hi, 0), slot_hot, NT, preferred_element_type=f32
        ) + lax.dot_general(jnp.concatenate(left_lo, 0), slot_hot, NT, preferred_element_type=f32)
        return 0

    lax.fori_loop(0, HELD // span, body, 0)
    for d in range(DEV):
        lo_d, hi_d = d % 64, d // 64
        at = slice(hi_d * SLOTS, (hi_d + 1) * SLOTS)
        send[d, 0:8, :] = acc[lo_d * 8 : lo_d * 8 + 8, at]
        send[d, 8:9, :] = acc[512 + lo_d : 513 + lo_d, at]


def scatter_phase(got, adj, group=8):
    adj[...] = jnp.zeros((LEVELS * ROWS, COLS), f32)
    span = group * SLOTS

    def body(g, _):
        g0 = g * group
        cells = jnp.concatenate([got[g0 + i, 8:9, :] for i in range(group)], 1).astype(i32)
        vals = jnp.concatenate([got[g0 + i, 0:8, :] for i in range(group)], 1)
        row = cells // COLS
        col_hot = one_hot(iota((COLS, span), 0) == cells - row * COLS)
        row_hot = one_hot(iota((ROWS, span), 0) == row)
        hi, lo = split2(vals)
        left_hi = jnp.concatenate([row_hot * hi[l : l + 1] for l in range(LEVELS)], 0)
        left_lo = jnp.concatenate([row_hot * lo[l : l + 1] for l in range(LEVELS)], 0)
        adj[...] += lax.dot_general(left_hi, col_hot, NT, preferred_element_type=f32) + lax.dot_general(
            left_lo, col_hot, NT, preferred_element_type=f32
        )
        return 0

    lax.fori_loop(0, DEV // group, body, 0)


def strip_sum(sq):
    return sq[:, :128] + sq[:, 128:]


def k_pass(src, dst, first, systems, halo_l, halo_r, cols_out, kd, cf, sums, which, own=None):
    def strip(i, _):
        r0 = pl.multiple_of(i * 8, 8)
        mid, below, above = (pl.multiple_of(r0 + k, 8) for k in (8, 16, 0))
        rows8, lane, row8 = iota((8, 256), 0), iota((8, 128), 1), None
        north, south, west, east = [cf[k, pl.ds(r0, 8), :] for k in range(4)]
        hl, hr = halo_l[pl.ds(r0, 8), :], halo_r[pl.ds(r0, 8), :]
        edge_l = edge_r = jnp.zeros((8, 128), f32)
        for l in range(LEVELS):
            diag = kd[l, pl.ds(r0, 8), :]
            for s in range(systems):
                j = s * LEVELS + l
                f = first + j
                c = src[f, pl.ds(mid, 8), :]
                up = pltpu.roll(jnp.where(rows8 == 7, src[f, pl.ds(above, 8), :], c), 1, 0)
                down = pltpu.roll(jnp.where(rows8 == 0, src[f, pl.ds(below, 8), :], c), 7, 0)
                cl, cr = c[:, :128], c[:, 128:]
                left = jnp.concatenate(
                    [
                        pltpu.roll(jnp.where(lane == 127, pltpu.roll(hl, 127 - j, 1), cl), 1, 1),
                        pltpu.roll(jnp.where(lane == 127, cl, cr), 1, 1),
                    ],
                    1,
                )
                right = jnp.concatenate(
                    [
                        pltpu.roll(jnp.where(lane == 0, cr, cl), 127, 1),
                        pltpu.roll(jnp.where(lane == 0, pltpu.roll(hr, (128 - j) % 128, 1), cr), 127, 1),
                    ],
                    1,
                )
                out = diag * c - north * up - south * down - west * left - east * right
                sums[which, f] += strip_sum(out * out)
                if own is not None:
                    sums[own, f] += strip_sum(c * c)
                if dst is not None:
                    dst[f, pl.ds(mid, 8), :] = out
                if cols_out is not None:
                    edge_l = jnp.where(lane == j, pltpu.roll(out[:, :128], j, 1), edge_l)
                    edge_r = jnp.where(lane == j, pltpu.roll(out[:, 128:], j + 1, 1), edge_r)
        if cols_out is not None:
            cols_out[0, pl.ds(r0, 8), :] = edge_r
            cols_out[1, pl.ds(r0, 8), :] = edge_l
        return 0

    lax.fori_loop(0, ROWS // 8, strip, 0)


def edges_of(field, first, count, rows_out, cols_out):
    def strip(i, _):
        r0 = pl.multiple_of(i * 8, 8)
        mid = pl.multiple_of(r0 + 8, 8)
        lane = iota((8, 128), 1)
        edge_l = edge_r = jnp.zeros((8, 128), f32)
        for j in range(count):
            c = field[first + j, pl.ds(mid, 8), :]
            edge_l = jnp.where(lane == j, pltpu.roll(c[:, :128], j, 1), edge_l)
            edge_r = jnp.where(lane == j, pltpu.roll(c[:, 128:], j + 1, 1), edge_r)
        cols_out[0, pl.ds(r0, 8), :] = edge_r
        cols_out[1, pl.ds(r0, 8), :] = edge_l
        return 0

    lax.fori_loop(0, ROWS // 8, strip, 0)
    rows_of(field, first, count, rows_out)


def rows_of(field, first, count, rows_out):
    for j in range(count):
        rows_out[0, j : j + 1, :] = field[first + j, ROWS + 7 : ROWS + 8, :]
        rows_out[1, j : j + 1, :] = field[first + j, 8:9, :]


def place_rows(field, first, count, rows_in):
    for j in range(count):
        field[first + j, 7:8, :] = rows_in[0, j : j + 1, :]
        field[first + j, ROWS + 8 : ROWS + 9, :] = rows_in[1, j : j + 1, :]


def lane_totals(sums, which, first, count):
    part = jnp.sum(sums[which, first : first + count], axis=1)
    total = jnp.sum(part, axis=1, keepdims=True)
    return jnp.sum(jnp.where(iota((count, 128), 1) == iota((count, 128), 0), total, 0.0), axis=0, keepdims=True)


def main_kernel(
    probes, kappa, cond_lat, cond_lon, inno, weight, dest, cell,
    image_out, adj_out, scale_out,
    v0, v1, v2, adj, acc, pos, carry, send, got, kd, cf, sums,
    prow_s, prow_r, pcol_s, pcol_r, arow_s, arow_r, acol_s, acol_r, ptot, atot,
    ready, a2a_s, a2a_r, px_s, px_r, ax_s, ax_r, pt_s, pt_r, at_s, at_r, out_sem,
):
    la, lo = lax.axis_index("lat"), lax.axis_index("lon")
    me = la * LON + lo
    lat_peers = [(lax.rem(la + i, LAT), lo) for i in range(1, LAT)]
    lon_peers = [(la, lax.rem(lo + i, LON)) for i in range(1, LON)]
    barrier = pltpu.get_barrier_semaphore()
    for peer in lat_peers + lon_peers:
        pl.semaphore_signal(barrier, inc=1, device_id=peer, device_id_type=MESH)

    beside = [lat_peers[0], lat_peers[-1], lon_peers[0], lon_peers[-1]]

    def exchange(rows_s, rows_r, cols_s, cols_r, s_sem, r_sem, k):
        parts = [(rows_s, rows_r, 0), (rows_s, rows_r, 1), (cols_s, cols_r, 0), (cols_s, cols_r, 1)]
        copies = []
        for n, (src, dst, side) in enumerate(parts):
            copies.append(
                pltpu.make_async_remote_copy(
                    src_ref=src.at[k, side], dst_ref=dst.at[k, side], send_sem=s_sem.at[k, n],
                    recv_sem=r_sem.at[k, n], device_id=beside[n], device_id_type=MESH,
                )
            )
            copies[-1].start()
        return copies

    def wait_all(copies):
        for copy in copies:
            copy.wait()

    def to_all(make):
        def start(i, _):
            make(lax.rem(me + i, DEV)).start()
            return 0

        def wait_sent(i, _):
            make(lax.rem(me + i, DEV)).wait_send()
            return 0

        def wait_got(i, _):
            make(lax.rem(me + i, DEV)).wait_recv()
            return 0

        lax.fori_loop(1, DEV, start, 0)
        return (lambda: lax.fori_loop(1, DEV, wait_sent, 0)), (lambda: lax.fori_loop(1, DEV, wait_got, 0))

    def broadcast(buf, s_sem, r_sem):
        def make(d):
            return pltpu.make_async_remote_copy(
                src_ref=buf.at[me], dst_ref=buf.at[me], send_sem=s_sem.at[d], recv_sem=r_sem.at[me],
                device_id=(d // LON, lax.rem(d, LON)), device_id_type=MESH,
            )

        def made(d):
            return pltpu.make_async_remote_copy(
                src_ref=buf.at[d], dst_ref=buf.at[d], send_sem=s_sem.at[d], recv_sem=r_sem.at[d],
                device_id=(d // LON, lax.rem(d, LON)), device_id_type=MESH,
            )

        return make, made

    sums[...] = jnp.zeros(sums.shape, f32)
    for j in range(NP):
        v0[j, 8 : 8 + ROWS, :] = probes[j].astype(f32)
    edges_of(v0, 0, NP, prow_s.at[0], pcol_s.at[0])
    prow_s[0, 0, NP : NP + 1, :] = cond_lat[ROWS - 1 : ROWS, :]
    lane = iota((ROWS, 128), 1)
    pcol_s[0, 0] = jnp.where(lane == NP, pltpu.roll(cond_lon[:, 128:], NP + 1, 1), pcol_s[0, 0])
    pl.semaphore_wait(barrier, LAT + LON - 2)
    for peer in lon_peers:
        pl.semaphore_signal(ready, inc=1, device_id=peer, device_id_type=MESH)
    copies = exchange(prow_s, prow_r, pcol_s, pcol_r, px_s, px_r, 0)

    rank_phase(dest, pos, carry)
    pack_phase(inno, weight, dest, cell, pos, acc, send)
    pl.semaphore_wait(ready, LON - 1)

    def station_copy(d):
        return pltpu.make_async_remote_copy(
            src_ref=send.at[d], dst_ref=got.at[me], send_sem=a2a_s.at[d], recv_sem=a2a_r.at[me],
            device_id=(d // LON, lax.rem(d, LON)), device_id_type=MESH,
        )

    def station_here(d):
        return pltpu.make_async_remote_copy(
            src_ref=send.at[d], dst_ref=got.at[d], send_sem=a2a_s.at[d], recv_sem=a2a_r.at[d],
            device_id=(d // LON, lax.rem(d, LON)), device_id_type=MESH,
        )

    def send_all(make):
        def start(i, _):
            make(lax.rem(me + i, DEV)).start()
            return 0

        lax.fori_loop(1, DEV, start, 0)

    def wait_for(made):
        def wait(i, _):
            made(lax.rem(me + i, DEV)).wait()
            return 0

        lax.fori_loop(1, DEV, wait, 0)

    send_all(station_copy)
    got[me] = send[me]

    wait_all(copies)
    row0 = iota((8, 256), 0) == 0
    inner = jnp.where(row0, 0.0, 1.0)
    lat_row = iota((ROWS, COLS), 0)
    south = jnp.where((lat_row == ROWS - 1) & (la == LAT - 1), 0.0, cond_lat[...])
    cf[1] = south
    up_row = jnp.where(la == 0, 0.0, prow_r[0, 0, NP : NP + 1, :])
    cf[0] = jnp.where(lat_row == 0, up_row, pltpu.roll(cond_lat[...], 1, 0))
    west_in = pltpu.roll(pcol_r[0, 0], 128 - NP, 1)
    el, er = cond_lon[:, :128], cond_lon[:, 128:]
    cf[2, :, :128] = jnp.where(lane == 0, west_in, pltpu.roll(el, 1, 1))
    cf[2, :, 128:] = pltpu.roll(jnp.where(lane == 127, el, er), 1, 1)
    cf[3] = cond_lon[...]
    for l in range(LEVELS):
        kd[l] = kappa[l] + cf[0] + cf[1] + cf[2] + cf[3]
    place_rows(v0, 0, NP, prow_r.at[0])
    k_pass(v0, v1, 0, 8, pcol_r.at[0, 0], pcol_r.at[0, 1], pcol_s.at[1], kd, cf, sums, 1, own=0)
    rows_of(v1, 0, NP, prow_s.at[1])
    copies = exchange(prow_s, prow_r, pcol_s, pcol_r, px_s, px_r, 1)
    wait_all(copies)
    place_rows(v1, 0, NP, prow_r.at[1])
    k_pass(v1, v2, 0, 8, pcol_r.at[1, 0], pcol_r.at[1, 1], pcol_s.at[2], kd, cf, sums, 2)
    rows_of(v2, 0, NP, prow_s.at[2])
    probe_copies = exchange(prow_s, prow_r, pcol_s, pcol_r, px_s, px_r, 2)
    probe_out = pltpu.make_async_copy(
        v2.at[pl.ds(0, NP), pl.ds(8, ROWS), :], image_out.at[pl.ds(0, NP)], out_sem.at[0]
    )
    probe_out.start()

    wait_for(station_here)
    scatter_phase(got, adj)
    for l in range(LEVELS):
        v0[NP + l, 8 : 8 + ROWS, :] = adj[l * ROWS : (l + 1) * ROWS, :]
    adj_copy = pltpu.make_async_copy(v0.at[pl.ds(NP, NA), pl.ds(8, ROWS), :], adj_out, out_sem.at[1])
    adj_copy.start()
    edges_of(v0, NP, NA, arow_s.at[0], acol_s.at[0])
    copies = exchange(arow_s, arow_r, acol_s, acol_r, ax_s, ax_r, 0)

    wait_all(probe_copies)
    place_rows(v2, 0, NP, prow_r.at[2])
    k_pass(v2, None, 0, 8, pcol_r.at[2, 0], pcol_r.at[2, 1], None, kd, cf, sums, 3)
    half = iota((1, 128), 1) < NP
    tot = [lane_totals(sums, k, 0, NP) for k in range(4)]
    ptot[me, 0:1, :] = jnp.where(half, tot[0], pltpu.roll(tot[1], NP, 1))
    ptot[me, 1:2, :] = jnp.where(half, tot[2], pltpu.roll(tot[3], NP, 1))
    p_make, p_made = broadcast(ptot, pt_s, pt_r)
    send_all(p_make)

    wait_all(copies)
    place_rows(v0, NP, NA, arow_r.at[0])
    k_pass(v0, v1, NP, 1, acol_r.at[0, 0], acol_r.at[0, 1], acol_s.at[1], kd, cf, sums, 1, own=0)
    rows_of(v1, NP, NA, arow_s.at[1])
    wait_all(exchange(arow_s, arow_r, acol_s, acol_r, ax_s, ax_r, 1))
    place_rows(v1, NP, NA, arow_r.at[1])
    k_pass(v1, v2, NP, 1, acol_r.at[1, 0], acol_r.at[1, 1], acol_s.at[2], kd, cf, sums, 2)
    rows_of(v2, NP, NA, arow_s.at[2])
    copies = exchange(arow_s, arow_r, acol_s, acol_r, ax_s, ax_r, 2)
    image_copy = pltpu.make_async_copy(
        v2.at[pl.ds(NP, NA), pl.ds(8, ROWS), :], image_out.at[pl.ds(NP, NA)], out_sem.at[2]
    )
    image_copy.start()
    wait_all(copies)
    place_rows(v2, NP, NA, arow_r.at[2])
    k_pass(v2, None, NP, 1, acol_r.at[2, 0], acol_r.at[2, 1], None, kd, cf, sums, 3)
    row = jnp.zeros((1, 128), f32)
    for k in range(4):
        row = row + pltpu.roll(lane_totals(sums, k, NP, NA), NA * k, 1)
    atot[me, 0:1, :] = row
    a_make, a_made = broadcast(atot, at_s, at_r)
    send_all(a_make)
    wait_for(p_made)
    wait_for(a_made)
    pt = jnp.sum(ptot[...], axis=0)
    at = jnp.sum(atot[...], axis=0)

    is_probe = iota((1, 128), 1) < NP
    ps = [pt[0:1], pltpu.roll(pt[0:1], NP, 1), pt[1:2], pltpu.roll(pt[1:2], NP, 1)]
    s0, s1, s2, s3 = [
        jnp.where(is_probe, ps[k], pltpu.roll(at, (NP - NA * k) % 128, 1)) for k in range(4)
    ]
    alpha = jnp.where(s1 > 0.0, s0 / s1, 0.0)
    next_rr = jnp.maximum(alpha * alpha * s2 - s0, 0.0)
    beta = jnp.where(s0 > 0.0, next_rr / s0, 0.0)
    grow = 1.0 + beta
    denom = grow * grow * s1 - 2.0 * grow * alpha * s2 + alpha * alpha * s3
    step = jnp.where(denom > 0.0, next_rr / denom, 0.0)
    step = jnp.minimum(jnp.maximum(step, STEP_MIN), STEP_MAX)
    scale_b, scale_q = alpha + step * grow, -alpha * step
    spot = iota((NF, 128), 1) == iota((NF, 128), 0)
    for k, scale in enumerate((scale_b, scale_q)):
        column = jnp.sum(jnp.where(spot, scale, 0.0), axis=1, keepdims=True)
        scale_out[k] = jnp.broadcast_to(column, (NF, 128))
    probe_out.wait()
    adj_copy.wait()
    image_copy.wait()


def final_kernel(probes, adj, image, scale, out):
    s = pl.program_id(0)

    def combine(field_of):
        for l in range(LEVELS):
            b = field_of(l)
            sb = scale[0, pl.ds(s * LEVELS + l, 1), :]
            sq = scale[1, pl.ds(s * LEVELS + l, 1), :]
            sb, sq = jnp.concatenate([sb, sb], 1), jnp.concatenate([sq, sq], 1)
            out[l] = sb * b + sq * image[l]

    @pl.when(s < 8)
    def _():
        combine(lambda l: probes[l].astype(f32))

    @pl.when(s == 8)
    def _():
        combine(lambda l: adj[l])


def local(probes, kappa, cond_lat, cond_lon, inno, weight, dest, cell):
    vmem = pl.BlockSpec(memory_space=pltpu.VMEM)
    hbm = pl.BlockSpec(memory_space=pl.ANY)
    reg, dma = pltpu.SemaphoreType.REGULAR, pltpu.SemaphoreType.DMA
    probes = probes.reshape(NP, ROWS, COLS)
    buf = lambda *shape: pltpu.VMEM(shape, f32)
    image, adj, scale = pl.pallas_call(
        main_kernel,
        out_shape=[
            jax.ShapeDtypeStruct((NF, ROWS, COLS), f32),
            jax.ShapeDtypeStruct((NA, ROWS, COLS), f32),
            jax.ShapeDtypeStruct((2, NF, 128), f32),
        ],
        in_specs=[vmem] * 8,
        out_specs=[hbm, hbm, vmem],
        scratch_shapes=[
            buf(NF, PAD, COLS), buf(NF, PAD, COLS), buf(NF, PAD, COLS),
            buf(LEVELS * ROWS, COLS), buf(576, 256), buf(1, HELD), buf(DEV, 128),
            buf(DEV, 9, 128), buf(DEV, 9, 128), buf(LEVELS, ROWS, COLS), buf(4, ROWS, COLS), buf(4, NF, 8, 128),
            buf(3, 2, NF, COLS), buf(3, 2, NF, COLS), buf(3, 2, ROWS, 128), buf(3, 2, ROWS, 128),
            buf(3, 2, NA, COLS), buf(3, 2, NA, COLS), buf(3, 2, ROWS, 128), buf(3, 2, ROWS, 128),
            buf(DEV, 2, 128), buf(DEV, 1, 128),
            reg, dma((DEV,)), dma((DEV,)), dma((3, 4)), dma((3, 4)), dma((3, 4)), dma((3, 4)),
            dma((DEV,)), dma((DEV,)), dma((DEV,)), dma((DEV,)), dma((3,)),
        ],
        compiler_params=pltpu.CompilerParams(
            collective_id=0, has_side_effects=True, vmem_limit_bytes=48 * 2**20
        ),
        name="main",
    )(
        probes, kappa, cond_lat, cond_lon, inno, weight.reshape(64, 128), dest.reshape(1, HELD), cell.reshape(64, 128)
    )
    out = pl.pallas_call(
        final_kernel,
        grid=(9,),
        out_shape=jax.ShapeDtypeStruct((NF, ROWS, COLS), f32),
        in_specs=[
            pl.BlockSpec((LEVELS, ROWS, COLS), lambda s: (jnp.minimum(s, 7), 0, 0)),
            pl.BlockSpec((NA, ROWS, COLS), lambda s: (0, 0, 0)),
            pl.BlockSpec((LEVELS, ROWS, COLS), lambda s: (s, 0, 0)),
            pl.BlockSpec((2, NF, 128), lambda s: (0, 0, 0)),
        ],
        out_specs=pl.BlockSpec((LEVELS, ROWS, COLS), lambda s: (s, 0, 0)),
        name="final",
    )(probes, adj, image, scale)
    return out.reshape(9, LEVELS, ROWS, COLS)


def solution(mesh):
    placed = (
        P(None, None, "lat", "lon"),
        P(None, "lat", "lon"),
        P("lat", "lon"),
        P("lat", "lon"),
        P(None, ("lat", "lon")),
        P(("lat", "lon")),
        P(("lat", "lon"), None),
        P(("lat", "lon")),
    )
    return jax.shard_map(
        local, mesh=mesh, in_specs=placed, out_specs=P(None, None, "lat", "lon"), check_vma=False
    )
```

time: 459 us -> 179 us (0.39); the launches traced: 450 us -> 178 us
  blocking collectives: 196 us -> 0 us
  Pallas kernels: 0 us -> 169 us
  other arithmetic: 97.4 us -> 0 us
  matrix products: 45.8 us -> 0 us
  starting transfers between devices: 43.8 us -> 0 us
  local copies, waits for them, and re-layouts: 43.3 us -> 8.95 us
  waiting for transfers between devices: 22.5 us -> 0 us
    psum x3 -> x0, blocking collectives: 196 us -> none  [the longest x2 129 us: norm_total(): return lax.psum(local_sum(resid * resid), ('lat', 'lon'))]
    pallas_call x0 -> x2, Pallas kernels: none -> 169 us  [the longest x1 161 us: local(): pl.pallas_call(main_kernel, out_shape=[jax.ShapeDtypeStruct((NF, ROWS, CO...]
    reduce_sum x5 -> x0, other arithmetic: 50.2 us -> none  [the longest x4 49.7 us: local_sum(): return jnp.sum(field, axis=(2, 3))]
    dot_general x3 -> x0, matrix products: 45.8 us -> none  [the longest x1 22.4 us: local(): adjoint = jnp.einsum('dlqr,dqc->lrc', placed, col_hot, precision=highest)]
    ppermute x15 -> x0, starting transfers between devices: 23.3 us -> none  [the longest x7 15.5 us: padded_2(): lax.ppermute(lax.slice_in_dim(block, 0, width, axis=dim), axis, backward)]
    slice x14 -> x0, local copies, waits for them, and re-layouts: 21.2 us -> none  [the longest x9 16.3 us: padded_2(): lax.slice_in_dim(block, block.shape[dim] - width, None, axis=dim)]
    all_to_all x2 -> x0, starting transfers between devices: 20.4 us -> none  [the longest x1 11.5 us: local(): lax.all_to_all(cell_slots, ('lat', 'lon'), split_axis=0, concat_axis=0, t...]
    ppermute x6 -> x0, local copies, waits for them, and re-layouts: 14.6 us -> none  [the longest x3 9.41 us: padded_2(): lax.ppermute(lax.slice_in_dim(block, 0, width, axis=dim), axis, backward)]
  transfers between devices with their start and end apart: 17 -> 0, of which waited for: 8 -> 0; matrix products, arithmetic and copies ran while one was open for 13% -> 0% of each run, Pallas kernels for 0% -> 0%
where the time goes in v1:
time: 179 us; the launch traced here: 178 us
  Pallas kernels  169 us (94%)
  local copies, waits for them, and re-layouts  8.95 us (5%)
    pallas_call x1, Pallas kernels, local(): pl.pallas_call(main_kernel, out_shape=[jax.ShapeDtypeStruct((NF, ROWS, CO...  161 us
    unnamed x20, local copies, waits for them, and re-layouts  8.95 us
    pallas_call x1, Pallas kernels, local(): pl.pallas_call(final_kernel, grid=(9,), out_shape=jax.ShapeDtypeStruct((N...  8.1 us

profile of v1, /device:TPU:1, one launch (start us, length us, event | category | flops | bytes accessed | tf_op | source)
XLA Modules:
  0.0 178.3 jit_solution(10122039185700065319)
XLA Ops:
  0.0 0.0 copy-start
  0.0 1.6 copy-done
  1.6 0.0 copy-start.1
  1.6 1.0 copy-done.1
  2.6 0.0 copy-start.3
  2.6 0.9 copy-done.3
  3.6 0.0 copy-start.5
  3.6 0.8 copy-done.5
  4.4 0.0 copy-start.6
  4.4 0.8 copy-done.6
  5.3 0.0 copy-start.7
  5.3 0.8 copy-done.7
  6.0 0.0 copy-start.8
  6.0 0.8 copy-done.8
  6.8 0.0 copy-start.9
  6.8 0.8 copy-done.9
  7.5 161.3 %main.1 = (f32[72,64,256]{2,1,0:T(8,128)}, f32[8,64,256]{2,1,0:T(8,128)S(1)}, f32[2,72,128]{2,1,0:T(8,128)S(1)}) custom-call(bf16[64,64,256]{2,1,0:T(8,128)(2,1)S(1)} %bitcast.6, f32[8,64,256]{2,1,0:T(8,128)S(1)} %copy-done.1, f32[64,256]{1,0:T(8,128)S(1)} %copy-done.5, f32[64,256]{1,0:T(8,128)S(1)} %copy-done.6, f32[8,8192]{1,0:T(8,128)S(1)} %copy-done.3, ...), custom_call_target="tpu_custom_call" | custom-call | tf_op jit(solution)/shard_map/main/pallas_call | solution.py:438
  168.8 0.0 copy-start.2
  168.8 0.8 copy-done.2
  169.6 0.0 copy-start.4
  169.6 0.6 copy-done.4
  170.2 8.1 %final.1 = f32[72,64,256]{2,1,0:T(8,128)} custom-call(bf16[64,64,256]{2,1,0:T(8,128)(2,1)} %bitcast.5, f32[8,64,256]{2,1,0:T(8,128)} %copy-done.2, f32[72,64,256]{2,1,0:T(8,128)} %get-tuple-element.9.image, f32[2,72,128]{2,1,0:T(8,128)} %copy-done.4), custom_call_target="tpu_custom_call" | custom-call | tf_op jit(solution)/shard_map/final/pallas_call | solution.py:464
Async XLA Ops:
  0.0 1.6 copy-start
  1.6 1.0 copy-start.1
  2.6 0.9 copy-start.3
  3.6 0.8 copy-start.5
  4.4 0.8 copy-start.6
  5.3 0.8 copy-start.7
  6.0 0.8 copy-start.8
  6.8 0.8 copy-start.9
  168.8 0.8 copy-start.2
  169.6 0.6 copy-start.4

commit v2 on v1

v2 whole, which is shorter than its diff:
```python
import functools

import jax
import jax.numpy as jnp
from jax import lax
from jax.experimental import pallas as pl
from jax.experimental.pallas import tpu as pltpu
from jax.sharding import PartitionSpec as P

f32, bf16, i32 = jnp.float32, jnp.bfloat16, jnp.int32
MESH = pl.DeviceIdType.MESH
LAT, LON, DEV = 8, 16, 128
LEVELS, ROWS, COLS = 8, 64, 256
NP, NA, NF = 64, 8, 72
PAD = ROWS + 16
HELD, SLOTS = 8192, 128
NT = (((1,), (1,)), ((), ()))
STEP_MIN, STEP_MAX = 1.0 / 25.0, 1.0 / 0.04


def iota(shape, dim):
    return lax.broadcasted_iota(i32, shape, dim)


def split2(v):
    hi = v.astype(bf16)
    return hi, (v - hi.astype(f32)).astype(bf16)


def one_hot(mask):
    return jnp.where(mask, 1.0, 0.0).astype(bf16)


def flat_rows(block, count):
    return jnp.concatenate([block[i : i + 1] for i in range(count)], 1)


def rank_phase(dest, pos, carry, span=256):
    upper = one_hot(iota((span, span), 0) < iota((span, span), 1))
    carry[...] = jnp.zeros((DEV, 128), f32)

    def body(c, _):
        s0 = pl.multiple_of(c * span, span)
        mask = iota((DEV, span), 0) == dest[:, pl.ds(s0, span)]
        hot = jnp.where(mask, 1.0, 0.0)
        within = jnp.dot(hot.astype(bf16), upper, preferred_element_type=f32)
        before = jnp.concatenate([carry[...]] * (span // 128), 1)
        pos[:, pl.ds(s0, span)] = jnp.sum(jnp.where(mask, within + before, 0.0), axis=0, keepdims=True)
        carry[...] += jnp.sum(hot, axis=1, keepdims=True)
        return 0

    lax.fori_loop(0, HELD // span, body, 0, unroll=4)


def pack_phase(inno, weight, dest, cell, pos, acc, send, span=1024):
    acc[...] = jnp.zeros((576, 256), f32)
    part = span // 128

    def body(c, _):
        s0 = pl.multiple_of(c * span, span)
        r0 = pl.multiple_of(c * part, part)
        d = dest[:, pl.ds(s0, span)]
        d_hi = jnp.where(d >= 64, 1, 0)
        d_lo = d - d_hi * 64
        slot = pos[:, pl.ds(s0, span)].astype(i32) + d_hi * SLOTS
        hi, lo = split2(inno[:, pl.ds(s0, span)] * flat_rows(weight[pl.ds(r0, part), :], part))
        cells = flat_rows(cell[pl.ds(r0, part), :], part)
        c_row = cells // COLS
        cell_hi = (c_row * COLS).astype(f32).astype(bf16)
        cell_lo = (cells - c_row * COLS).astype(f32).astype(bf16)
        slot_hot = one_hot(iota((256, span), 0) == slot)
        hi2, lo2 = jnp.concatenate([hi, hi], 0), jnp.concatenate([lo, lo], 0)
        pair = iota((16, span), 0) // 8
        left_hi, left_lo = [], []
        for t in range(32):
            mine = one_hot((pair + 2 * t) == d_lo)
            left_hi.append(mine * hi2)
            left_lo.append(mine * lo2)
        mine = one_hot(iota((64, span), 0) == d_lo)
        left_hi.append(mine * cell_hi)
        left_lo.append(mine * cell_lo)
        acc[...] += lax.dot_general(
            jnp.concatenate(left_hi, 0), slot_hot, NT, preferred_element_type=f32
        ) + lax.dot_general(jnp.concatenate(left_lo, 0), slot_hot, NT, preferred_element_type=f32)
        return 0

    lax.fori_loop(0, HELD // span, body, 0)
    for d in range(DEV):
        lo_d, hi_d = d % 64, d // 64
        at = slice(hi_d * SLOTS, (hi_d + 1) * SLOTS)
        send[d, 0:8, :] = acc[lo_d * 8 : lo_d * 8 + 8, at]
        send[d, 8:9, :] = acc[512 + lo_d : 513 + lo_d, at]


def scatter_phase(got, adj, arrived, group=8):
    adj[...] = jnp.zeros((LEVELS * ROWS, COLS), f32)
    span = group * SLOTS

    def body(g, _):
        sources = arrived(g)
        cells = jnp.concatenate([got[d, 8:9, :] for d in sources], 1).astype(i32)
        vals = jnp.concatenate([got[d, 0:8, :] for d in sources], 1)
        row = cells // COLS
        col_hot = one_hot(iota((COLS, span), 0) == cells - row * COLS)
        row_hot = one_hot(iota((ROWS, span), 0) == (row % 8) * 8 + row // 8)
        hi, lo = split2(vals)
        left_hi = jnp.concatenate([row_hot * hi[l : l + 1] for l in range(LEVELS)], 0)
        left_lo = jnp.concatenate([row_hot * lo[l : l + 1] for l in range(LEVELS)], 0)
        adj[...] += lax.dot_general(left_hi, col_hot, NT, preferred_element_type=f32) + lax.dot_general(
            left_lo, col_hot, NT, preferred_element_type=f32
        )
        return 0

    lax.fori_loop(0, DEV // group, body, 0)


def put_swapped(ref, values):
    for h in range(2):
        for a in range(8):
            ref[h, pl.ds(a, 8, stride=8), :] = values[a * 8 : a * 8 + 8, h * 128 : h * 128 + 128]


def strip_sum(sq):
    return sq[:, :128] + sq[:, 128:]


def k_pass(src, dst, first, span, halo, kd, cf, sums, which, own=None):
    def strip(i, _):
        r0 = pl.multiple_of(i * 8, 8)
        mid, below, above = (pl.multiple_of(r0 + k, 8) for k in (8, 16, 0))
        lane = iota((8, 128), 1)
        at_0, at_127 = lane == 0, lane == 127
        wide = lambda ref, k, at: jnp.concatenate([ref[k, 0, at, :], ref[k, 1, at, :]], 1)
        here = pl.ds(r0, 8)
        north, south, west, east = [wide(cf, k, here) for k in range(4)]
        for n in span:
            f = first + n
            c = wide(src, f, pl.ds(mid, 8))
            cl, cr, beyond = c[:, :128], c[:, 128:], halo[n, here, :]
            left = jnp.concatenate(
                [pltpu.roll(jnp.where(at_127, beyond, cl), 1, 1), pltpu.roll(jnp.where(at_127, cl, cr), 1, 1)], 1
            )
            right = jnp.concatenate(
                [pltpu.roll(jnp.where(at_0, cr, cl), 127, 1), pltpu.roll(jnp.where(at_0, beyond, cr), 127, 1)], 1
            )
            up, down = wide(src, f, pl.ds(above, 8)), wide(src, f, pl.ds(below, 8))
            out = wide(kd, n % 8, here) * c - north * up - south * down - west * left - east * right
            sums[which, f] += strip_sum(out * out)
            if own is not None:
                sums[own, f] += strip_sum(c * c)
            if dst is not None:
                dst[f, 0, pl.ds(mid, 8), :] = out[:, :128]
                dst[f, 1, pl.ds(mid, 8), :] = out[:, 128:]
        return 0

    lax.fori_loop(0, ROWS // 8, strip, 0)


def cols_of(field, first, count, cols_out):
    def strip(i, _):
        r0 = pl.multiple_of(i * 8, 8)
        mid = pl.multiple_of(r0 + 8, 8)
        lane = iota((8, 128), 1)
        edge_l = edge_r = jnp.zeros((8, 128), f32)
        for j in range(count):
            edge_l = jnp.where(lane == j, pltpu.roll(field[first + j, 0, pl.ds(mid, 8), :], j, 1), edge_l)
            edge_r = jnp.where(lane == j, pltpu.roll(field[first + j, 1, pl.ds(mid, 8), :], j + 1, 1), edge_r)
        cols_out[0, pl.ds(r0, 8), :] = edge_r
        cols_out[1, pl.ds(r0, 8), :] = edge_l
        return 0

    lax.fori_loop(0, ROWS // 8, strip, 0)


def place_cols(halo, count, cols_in):
    def strip(i, _):
        here = pl.ds(pl.multiple_of(i * 8, 8), 8)
        lane = iota((8, 128), 1)
        before, after = cols_in[0, here, :], cols_in[1, here, :]
        for j in range(count):
            halo[j, here, :] = jnp.where(
                lane == 127, pltpu.roll(before, 127 - j, 1), pltpu.roll(after, (128 - j) % 128, 1)
            )
        return 0

    lax.fori_loop(0, ROWS // 8, strip, 0)


def rows_of(field, first, count, rows_out):
    for j in range(count):
        for h in range(2):
            at = slice(h * 128, h * 128 + 128)
            rows_out[0, j : j + 1, at] = field[first + j, h, ROWS + 7 : ROWS + 8, :]
            rows_out[1, j : j + 1, at] = field[first + j, h, 8:9, :]


def place_rows(field, first, count, rows_in):
    row = iota((8, 128), 0)
    for j in range(count):
        f = first + j
        for h in range(2):
            at = slice(h * 128, h * 128 + 128)
            last, top = field[f, h, ROWS : ROWS + 8, :], field[f, h, 8:16, :]
            field[f, h, 0:8, :] = jnp.where(row == 0, rows_in[0, j : j + 1, at], pltpu.roll(last, 1, 0))
            field[f, h, ROWS + 8 : ROWS + 16, :] = jnp.where(
                row == 7, rows_in[1, j : j + 1, at], pltpu.roll(top, 7, 0)
            )


def lane_totals(sums, which, first, count):
    part = jnp.sum(sums[which, first : first + count], axis=1)
    total = jnp.sum(part, axis=1, keepdims=True)
    return jnp.sum(jnp.where(iota((count, 128), 1) == iota((count, 128), 0), total, 0.0), axis=0, keepdims=True)


def main_kernel(
    probes_in, kappa_in, cond_lat_in, cond_lon_in, inno_in, weight_in, dest_in, cell_in,
    v0, v2, scale_out,
    v1, adj, acc, pos, carry, send, got, kd, cf, sums,
    prow_s, prow_r, pcol_s, pcol_r, arow_s, arow_r, acol_s, acol_r, tot, phalo, ahalo,
    ready, a2a_s, a2a_r, px_s, px_r, ax_s, ax_r, tot_s, tot_r,
    probes, kappa, cond_lat, cond_lon, inno, weight, dest, cell, in_sem,
):
    la, lo = lax.axis_index("lat"), lax.axis_index("lon")
    me = la * LON + lo
    ins = [
        pltpu.make_async_copy(src, dst, in_sem.at[k])
        for k, (src, dst) in enumerate(
            [
                (probes_in, probes), (cond_lat_in, cond_lat), (cond_lon_in, cond_lon), (dest_in, dest),
                (weight_in, weight), (cell_in, cell), (inno_in, inno), (kappa_in, kappa),
            ]
        )
    ]
    for copy in ins:
        copy.start()
    lat_peers = [(lax.rem(la + i, LAT), lo) for i in range(1, LAT)]
    lon_peers = [(la, lax.rem(lo + i, LON)) for i in range(1, LON)]
    barrier = pltpu.get_barrier_semaphore()
    for peer in lat_peers + lon_peers:
        pl.semaphore_signal(barrier, inc=1, device_id=peer, device_id_type=MESH)

    beside = [lat_peers[0], lat_peers[-1], lon_peers[0], lon_peers[-1]]

    def exchange(rows_s, rows_r, cols_s, cols_r, s_sem, r_sem, k):
        parts = [(rows_s, rows_r, 0), (rows_s, rows_r, 1), (cols_s, cols_r, 0), (cols_s, cols_r, 1)]
        copies = []
        for n, (src, dst, side) in enumerate(parts):
            copies.append(
                pltpu.make_async_remote_copy(
                    src_ref=src.at[k, side], dst_ref=dst.at[k, side], send_sem=s_sem.at[k, n],
                    recv_sem=r_sem.at[k, n], device_id=beside[n], device_id_type=MESH,
                )
            )
            copies[-1].start()
        return copies

    def wait_all(copies):
        for copy in copies:
            copy.wait()

    x, y, z, core = lo // 4, la // 2, lax.rem(lo, 4), lax.rem(la, 2)

    def step_of(a):
        return a + a // 2 - 2 * (a // 3)

    def group_of(g):
        gy, gx = lax.rem(y + step_of(g // 4), 4), lax.rem(x + step_of(lax.rem(g, 4)), 4)
        return [(gy * 2 + lax.rem(core + c, 2)) * LON + gx * 4 + lax.rem(z + dz, 4) for c in range(2) for dz in range(4)]

    def device(d):
        return (d // LON, lax.rem(d, LON))

    def to_all(make):
        for d in group_of(0)[1:]:
            make(d).start()

        def rest(g, _):
            for d in group_of(g):
                make(d).start()
            return 0

        lax.fori_loop(1, DEV // 8, rest, 0)

    def station_copy(src, dst):
        return pltpu.make_async_remote_copy(
            src_ref=send.at[src], dst_ref=got.at[dst], send_sem=a2a_s, recv_sem=a2a_r.at[dst],
            device_id=device(src), device_id_type=MESH,
        )

    def total_copy(d):
        return pltpu.make_async_remote_copy(
            src_ref=tot.at[me], dst_ref=tot.at[me], send_sem=tot_s, recv_sem=tot_r,
            device_id=device(d), device_id_type=MESH,
        )

    sums[...] = jnp.zeros(sums.shape, f32)
    for copy in ins[:3]:
        copy.wait()

    def widen(s, _):
        for l in range(LEVELS):
            f = s * LEVELS + l
            for a in range(4):
                wide = probes[f, a * 16 : a * 16 + 16, :].astype(f32)
                for h in range(2):
                    at = slice(h * 128, h * 128 + 128)
                    v0[f, h, pl.ds(8 + 2 * a, 8, stride=8), :] = wide[:8, at]
                    v0[f, h, pl.ds(9 + 2 * a, 8, stride=8), :] = wide[8:, at]
        return 0

    lax.fori_loop(0, 8, widen, 0)
    cols_of(v0, 0, NP, pcol_s.at[0])
    rows_of(v0, 0, NP, prow_s.at[0])
    lane = iota((ROWS, 128), 1)
    lat_row = iota((ROWS, COLS), 0)
    prow_s[0, 0, NP : NP + 1, :] = cond_lat[ROWS - 1 : ROWS, :]
    put_swapped(cf.at[3], cond_lon[...])
    pcol_s[0, 0] = jnp.where(lane == NP, pltpu.roll(cf[3, 1], NP + 1, 1), pcol_s[0, 0])

    for copy in ins[3:]:
        copy.wait()
    rank_phase(dest, pos, carry)
    pack_phase(inno, weight, dest, cell, pos, acc, send)
    pl.semaphore_wait(barrier, LAT + LON - 2)
    for peer in lon_peers:
        pl.semaphore_signal(ready, inc=1, device_id=peer, device_id_type=MESH)
    copies = exchange(prow_s, prow_r, pcol_s, pcol_r, px_s, px_r, 0)
    got[me] = send[me]
    pl.semaphore_wait(ready, LON - 1)
    to_all(lambda d: station_copy(d, me))

    wait_all(copies)
    put_swapped(
        cf.at[0],
        jnp.where(
            lat_row == 0, jnp.where(la == 0, 0.0, prow_r[0, 0, NP : NP + 1, :]), pltpu.roll(cond_lat[...], 1, 0)
        ),
    )
    put_swapped(cf.at[1], jnp.where((lat_row == ROWS - 1) & (la == LAT - 1), 0.0, cond_lat[...]))
    el, er = cf[3, 0], cf[3, 1]
    cf[2, 0] = jnp.where(lane == 0, pltpu.roll(pcol_r[0, 0], 128 - NP, 1), pltpu.roll(el, 1, 1))
    cf[2, 1] = pltpu.roll(jnp.where(lane == 127, el, er), 1, 1)
    faces = cf[0] + cf[1] + cf[2] + cf[3]
    for l in range(LEVELS):
        put_swapped(kd.at[l], kappa[l])
        kd[l] += faces
    all_p, all_a = range(NP), range(NA)
    place_rows(v0, 0, NP, prow_r.at[0])
    place_cols(phalo, NP, pcol_r.at[0])
    k_pass(v0, v1, 0, all_p, phalo, kd, cf, sums, 1, own=0)
    cols_of(v1, 0, NP, pcol_s.at[1])
    rows_of(v1, 0, NP, prow_s.at[1])
    probe_copies = exchange(prow_s, prow_r, pcol_s, pcol_r, px_s, px_r, 1)

    def arrived(g):
        sources = group_of(g)
        for n, d in enumerate(sources):
            if n:
                station_copy(d, d).wait_recv()
            else:

                @pl.when(g > 0)
                def _():
                    station_copy(d, d).wait_recv()

        return sources

    scatter_phase(got, adj, arrived)
    for l in range(LEVELS):
        for h in range(2):
            v0[NP + l, h, 8 : 8 + ROWS, :] = adj[l * ROWS : (l + 1) * ROWS, h * 128 : h * 128 + 128]
    cols_of(v0, NP, NA, acol_s.at[0])
    rows_of(v0, NP, NA, arow_s.at[0])
    copies = exchange(arow_s, arow_r, acol_s, acol_r, ax_s, ax_r, 0)

    wait_all(probe_copies)
    place_rows(v1, 0, NP, prow_r.at[1])
    place_cols(phalo, NP, pcol_r.at[1])
    k_pass(v1, v2, 0, all_p, phalo, kd, cf, sums, 2)
    cols_of(v2, 0, NP, pcol_s.at[2])
    rows_of(v2, 0, NP, prow_s.at[2])
    probe_copies = exchange(prow_s, prow_r, pcol_s, pcol_r, px_s, px_r, 2)
    wait_all(copies)
    place_rows(v0, NP, NA, arow_r.at[0])
    place_cols(ahalo, NA, acol_r.at[0])
    k_pass(v0, v1, NP, all_a, ahalo, kd, cf, sums, 1, own=0)
    cols_of(v1, NP, NA, acol_s.at[1])
    rows_of(v1, NP, NA, arow_s.at[1])
    copies = exchange(arow_s, arow_r, acol_s, acol_r, ax_s, ax_r, 1)
    wait_all(probe_copies)
    place_rows(v2, 0, NP, prow_r.at[2])
    place_cols(phalo, NP, pcol_r.at[2])
    k_pass(v2, None, 0, range(32), phalo, kd, cf, sums, 3)
    wait_all(copies)
    place_rows(v1, NP, NA, arow_r.at[1])
    place_cols(ahalo, NA, acol_r.at[1])
    k_pass(v1, v2, NP, all_a, ahalo, kd, cf, sums, 2)
    cols_of(v2, NP, NA, acol_s.at[2])
    rows_of(v2, NP, NA, arow_s.at[2])
    copies = exchange(arow_s, arow_r, acol_s, acol_r, ax_s, ax_r, 2)
    k_pass(v2, None, 0, range(32, NP), phalo, kd, cf, sums, 3)
    half = iota((1, 128), 1) < NP
    part = [lane_totals(sums, k, 0, NP) for k in range(4)]
    tot[me, 0:1, :] = jnp.where(half, part[0], pltpu.roll(part[1], NP, 1))
    tot[me, 1:2, :] = jnp.where(half, part[2], pltpu.roll(part[3], NP, 1))
    tot[me, 3:4, :] = jnp.zeros((1, 128), f32)
    wait_all(copies)
    place_rows(v2, NP, NA, arow_r.at[2])
    place_cols(ahalo, NA, acol_r.at[2])
    k_pass(v2, None, NP, all_a, ahalo, kd, cf, sums, 3)
    row = jnp.zeros((1, 128), f32)
    for k in range(4):
        row = row + pltpu.roll(lane_totals(sums, k, NP, NA), NA * k, 1)
    tot[me, 2:3, :] = row

    to_all(total_copy)
    others = pltpu.make_async_remote_copy(
        src_ref=send.at[pl.ds(0, DEV - 1)], dst_ref=got.at[pl.ds(0, DEV - 1)], send_sem=a2a_s, recv_sem=tot_r,
        device_id=lon_peers[0], device_id_type=MESH,
    )
    others.wait_send()
    others = pltpu.make_async_remote_copy(
        src_ref=tot.at[pl.ds(0, DEV - 1)], dst_ref=tot.at[pl.ds(0, DEV - 1)], send_sem=tot_s, recv_sem=tot_r,
        device_id=lon_peers[0], device_id_type=MESH,
    )
    others.wait()
    total = jnp.sum(tot[...], axis=0)
    pt, at = total[0:2], total[2:3]

    is_probe = iota((1, 128), 1) < NP
    ps = [pt[0:1], pltpu.roll(pt[0:1], NP, 1), pt[1:2], pltpu.roll(pt[1:2], NP, 1)]
    s0, s1, s2, s3 = [
        jnp.where(is_probe, ps[k], pltpu.roll(at, (NP - NA * k) % 128, 1)) for k in range(4)
    ]
    alpha = jnp.where(s1 > 0.0, s0 / s1, 0.0)
    next_rr = jnp.maximum(alpha * alpha * s2 - s0, 0.0)
    beta = jnp.where(s0 > 0.0, next_rr / s0, 0.0)
    grow = 1.0 + beta
    denom = grow * grow * s1 - 2.0 * grow * alpha * s2 + alpha * alpha * s3
    step = jnp.where(denom > 0.0, next_rr / denom, 0.0)
    step = jnp.minimum(jnp.maximum(step, STEP_MIN), STEP_MAX)
    scale_b, scale_q = alpha + step * grow, -alpha * step
    spot = iota((NF, 128), 1) == iota((NF, 128), 0)
    for k, scale in enumerate((scale_b, scale_q)):
        column = jnp.sum(jnp.where(spot, scale, 0.0), axis=1, keepdims=True)
        scale_out[k] = jnp.broadcast_to(column, (NF, 128))


def final_kernel(v0, v2, scale, out, block, sem):
    def copy(s, h):
        return pltpu.make_async_copy(block.at[s, :, h], out.at[s, :, :, pl.ds(h * 128, 128)], sem.at[s, h])

    def system(s, _):
        for h in range(2):
            for l in range(LEVELS):
                f = s * LEVELS + l
                sb, sq = scale[0, pl.ds(f, 1), :], scale[1, pl.ds(f, 1), :]
                for t in range(8):
                    at = pl.ds(8 + 8 * t, 8)
                    block[s, l, h, pl.ds(t, 8, stride=8), :] = sb * v0[f, h, at, :] + sq * v2[f, h, at, :]
            copy(s, h).start()
        return 0

    def wait(s, _):
        for h in range(2):
            copy(s, h).wait()
        return 0

    lax.fori_loop(0, 9, system, 0)
    lax.fori_loop(0, 9, wait, 0)


def local(probes, kappa, cond_lat, cond_lon, inno, weight, dest, cell):
    vmem = pl.BlockSpec(memory_space=pltpu.VMEM)
    hbm = pl.BlockSpec(memory_space=pltpu.HBM)
    reg, dma = pltpu.SemaphoreType.REGULAR, pltpu.SemaphoreType.DMA
    probes = probes.reshape(NP, ROWS, COLS)
    weight, cell, dest = weight.reshape(64, 128), cell.reshape(64, 128), dest.reshape(1, HELD)
    args = (probes, kappa, cond_lat, cond_lon, inno, weight, dest, cell)
    buf = lambda *shape: pltpu.VMEM(shape, f32)
    v0, v2, scale = pl.pallas_call(
        main_kernel,
        out_shape=[
            pltpu.VMEM((NF, 2, PAD, 128), f32),
            pltpu.VMEM((NF, 2, PAD, 128), f32),
            pltpu.VMEM((2, NF, 128), f32),
        ],
        in_specs=[hbm] * 8,
        out_specs=[vmem] * 3,
        scratch_shapes=[
            buf(NF, 2, PAD, 128),
            buf(LEVELS * ROWS, COLS), buf(576, 256), buf(1, HELD), buf(DEV, 128),
            buf(DEV, 9, 128), buf(DEV, 9, 128), buf(LEVELS, 2, ROWS, 128), buf(4, 2, ROWS, 128), buf(4, NF, 8, 128),
            buf(3, 2, NF, COLS), buf(3, 2, NF, COLS), buf(3, 2, ROWS, 128), buf(3, 2, ROWS, 128),
            buf(3, 2, NA, COLS), buf(3, 2, NA, COLS), buf(3, 2, ROWS, 128), buf(3, 2, ROWS, 128),
            buf(DEV, 4, 128), buf(NP, ROWS, 128), buf(NA, ROWS, 128),
            reg, dma, dma((DEV,)), dma((3, 4)), dma((3, 4)), dma((3, 4)), dma((3, 4)), dma, dma,
            *[pltpu.VMEM(a.shape, a.dtype) for a in args],
            dma((8,)),
        ],
        compiler_params=pltpu.CompilerParams(
            collective_id=0, has_side_effects=True, vmem_limit_bytes=36 * 2**20
        ),
        name="main",
    )(*[pltpu.with_memory_space_constraint(a, pltpu.HBM) for a in args])
    out = pl.pallas_call(
        final_kernel,
        out_shape=jax.ShapeDtypeStruct((9, LEVELS, ROWS, COLS), f32),
        in_specs=[vmem] * 3,
        out_specs=hbm,
        scratch_shapes=[buf(9, LEVELS, 2, ROWS, 128), dma((9, 2))],
        compiler_params=pltpu.CompilerParams(vmem_limit_bytes=12 * 2**20),
        name="final",
    )(v0, v2, scale)
    return out


def solution(mesh):
    placed = (
        P(None, None, "lat", "lon"),
        P(None, "lat", "lon"),
        P("lat", "lon"),
        P("lat", "lon"),
        P(None, ("lat", "lon")),
        P(("lat", "lon")),
        P(("lat", "lon"), None),
        P(("lat", "lon")),
    )
    return jax.shard_map(
        local, mesh=mesh, in_specs=placed, out_specs=P(None, None, "lat", "lon"), check_vma=False
    )
```

time: 179 us -> 76.8 us (0.43)
  Pallas kernels: 169 us -> 76.6 us
  local copies, waits for them, and re-layouts: 8.95 us -> 0 us
    pallas_call x2, Pallas kernels: 169 us -> 76.6 us  [the longest x1 74.3 us: local(): pl.pallas_call(main_kernel, out_shape=[pltpu.VMEM((NF, 2, PAD, 128), f32)...]
    unnamed x20 -> x0, local copies, waits for them, and re-layouts: 8.95 us -> none
where the time goes in v2:
time: 76.8 us; the launch traced here: 76.6 us
  Pallas kernels  76.6 us (100%)
    pallas_call x1, Pallas kernels, local(): pl.pallas_call(main_kernel, out_shape=[pltpu.VMEM((NF, 2, PAD, 128), f32)...  74.3 us
    pallas_call x1, Pallas kernels, local(): pl.pallas_call(final_kernel, out_shape=jax.ShapeDtypeStruct((9, LEVELS, R...  2.37 us

profile of v2, /device:TPU:1, one launch (start us, length us, event | category | flops | bytes accessed | tf_op | source)
XLA Modules:
  0.0 76.6 jit_solution(4778350688353748879)
XLA Ops:
  0.0 74.3 %main.1 = (f32[72,2,80,128]{3,2,1,0:T(8,128)S(1)}, f32[72,2,80,128]{3,2,1,0:T(8,128)S(1)}, f32[2,72,128]{2,1,0:T(8,128)S(1)}) custom-call(bf16[64,64,256]{2,1,0:T(8,128)(2,1)} %bitcast.4, f32[8,64,256]{2,1,0:T(8,128)} %kappa_in.1, f32[64,256]{1,0:T(8,128)} %cond_lat_in.1, f32[64,256]{1,0:T(8,128)} %cond_lon_in.1, f32[8,8192]{1,0:T(8,128)} %inno_in.1, ...), custom_call_target="tpu_custom_call" | custom-call | tf_op jit(solution)/shard_map/main/pallas_call | solution.py:482
  74.3 2.4 %final.1 = f32[9,8,64,256]{3,2,1,0:T(8,128)} custom-call(f32[72,2,80,128]{3,2,1,0:T(8,128)S(1)} %get-tuple-element.8.v0, f32[72,2,80,128]{3,2,1,0:T(8,128)S(1)} %get-tuple-element.9.v2, f32[2,72,128]{2,1,0:T(8,128)S(1)} %get-tuple-element.10.scale), custom_call_target="tpu_custom_call" | custom-call | tf_op jit(solution)/shard_map/final/pallas_call | solution.py:507

commit v3 on v2

--- a/solution.py
+++ b/solution.py
@@ -15,6 +15,7 @@
 PAD = ROWS + 16
 HELD, SLOTS = 8192, 128
 NT = (((1,), (1,)), ((), ()))
+EARLY = 8
 STEP_MIN, STEP_MAX = 1.0 / 25.0, 1.0 / 0.04
 
 
@@ -92,8 +93,7 @@
         send[d, 8:9, :] = acc[512 + lo_d : 513 + lo_d, at]
 
 
-def scatter_phase(got, adj, arrived, group=8):
-    adj[...] = jnp.zeros((LEVELS * ROWS, COLS), f32)
+def scatter_phase(got, adj, arrived, first, last, group=8):
     span = group * SLOTS
 
     def body(g, _):
@@ -111,7 +111,7 @@
         )
         return 0
 
-    lax.fori_loop(0, DEV // group, body, 0)
+    lax.fori_loop(first, last, body, 0)
 
 
 def put_swapped(ref, values):
@@ -153,7 +153,7 @@
                 dst[f, 1, pl.ds(mid, 8), :] = out[:, 128:]
         return 0
 
-    lax.fori_loop(0, ROWS // 8, strip, 0)
+    lax.fori_loop(0, ROWS // 8, strip, 0, unroll=len(span) <= NA)
 
 
 def cols_of(field, first, count, cols_out):
@@ -169,7 +169,7 @@
         cols_out[1, pl.ds(r0, 8), :] = edge_l
         return 0
 
-    lax.fori_loop(0, ROWS // 8, strip, 0)
+    lax.fori_loop(0, ROWS // 8, strip, 0, unroll=count <= NA)
 
 
 def place_cols(halo, count, cols_in):
@@ -183,7 +183,7 @@
             )
         return 0
 
-    lax.fori_loop(0, ROWS // 8, strip, 0)
+    lax.fori_loop(0, ROWS // 8, strip, 0, unroll=count <= NA)
 
 
 def rows_of(field, first, count, rows_out):
@@ -321,11 +321,11 @@
     for copy in ins[3:]:
         copy.wait()
     rank_phase(dest, pos, carry)
-    pack_phase(inno, weight, dest, cell, pos, acc, send)
     pl.semaphore_wait(barrier, LAT + LON - 2)
     for peer in lon_peers:
         pl.semaphore_signal(ready, inc=1, device_id=peer, device_id_type=MESH)
     copies = exchange(prow_s, prow_r, pcol_s, pcol_r, px_s, px_r, 0)
+    pack_phase(inno, weight, dest, cell, pos, acc, send)
     got[me] = send[me]
     pl.semaphore_wait(ready, LON - 1)
     to_all(lambda d: station_copy(d, me))
@@ -366,14 +366,8 @@
 
         return sources
 
-    scatter_phase(got, adj, arrived)
-    for l in range(LEVELS):
-        for h in range(2):
-            v0[NP + l, h, 8 : 8 + ROWS, :] = adj[l * ROWS : (l + 1) * ROWS, h * 128 : h * 128 + 128]
-    cols_of(v0, NP, NA, acol_s.at[0])
-    rows_of(v0, NP, NA, arow_s.at[0])
-    copies = exchange(arow_s, arow_r, acol_s, acol_r, ax_s, ax_r, 0)
-
+    adj[...] = jnp.zeros((LEVELS * ROWS, COLS), f32)
+    scatter_phase(got, adj, arrived, 0, EARLY)
     wait_all(probe_copies)
     place_rows(v1, 0, NP, prow_r.at[1])
     place_cols(phalo, NP, pcol_r.at[1])
@@ -381,6 +375,18 @@
     cols_of(v2, 0, NP, pcol_s.at[2])
     rows_of(v2, 0, NP, prow_s.at[2])
     probe_copies = exchange(prow_s, prow_r, pcol_s, pcol_r, px_s, px_r, 2)
+    scatter_phase(got, adj, arrived, EARLY, DEV // 8)
+    for l in range(LEVELS):
+        for h in range(2):
+            v0[NP + l, h, 8 : 8 + ROWS, :] = adj[l * ROWS : (l + 1) * ROWS, h * 128 : h * 128 + 128]
+    cols_of(v0, NP, NA, acol_s.at[0])
+    rows_of(v0, NP, NA, arow_s.at[0])
+    copies = exchange(arow_s, arow_r, acol_s, acol_r, ax_s, ax_r, 0)
+
+    wait_all(probe_copies)
+    place_rows(v2, 0, NP, prow_r.at[2])
+    place_cols(phalo, NP, pcol_r.at[2])
+    k_pass(v2, None, 0, range(32), phalo, kd, cf, sums, 3)
     wait_all(copies)
     place_rows(v0, NP, NA, arow_r.at[0])
     place_cols(ahalo, NA, acol_r.at[0])
@@ -388,10 +394,7 @@
     cols_of(v1, NP, NA, acol_s.at[1])
     rows_of(v1, NP, NA, arow_s.at[1])
     copies = exchange(arow_s, arow_r, acol_s, acol_r, ax_s, ax_r, 1)
-    wait_all(probe_copies)
-    place_rows(v2, 0, NP, prow_r.at[2])
-    place_cols(phalo, NP, pcol_r.at[2])
-    k_pass(v2, None, 0, range(32), phalo, kd, cf, sums, 3)
+    k_pass(v2, None, 0, range(32, NP), phalo, kd, cf, sums, 3)
     wait_all(copies)
     place_rows(v1, NP, NA, arow_r.at[1])
     place_cols(ahalo, NA, acol_r.at[1])
@@ -399,7 +402,6 @@
     cols_of(v2, NP, NA, acol_s.at[2])
     rows_of(v2, NP, NA, arow_s.at[2])
     copies = exchange(arow_s, arow_r, acol_s, acol_r, ax_s, ax_r, 2)
-    k_pass(v2, None, 0, range(32, NP), phalo, kd, cf, sums, 3)
     half = iota((1, 128), 1) < NP
     part = [lane_totals(sums, k, 0, NP) for k in range(4)]
     tot[me, 0:1, :] = jnp.where(half, part[0], pltpu.roll(part[1], NP, 1))

time: 76.8 us -> 72.3 us (0.941)
  Pallas kernels: 76.6 us -> 72.2 us
    pallas_call x1, Pallas kernels: 74.3 us -> 69.8 us  [local(): pl.pallas_call(main_kernel, out_shape=[pltpu.VMEM((NF, 2, PAD, 128), f32)...]
where the time goes in v3:
time: 72.3 us; the launch traced here: 72.2 us
  Pallas kernels  72.2 us (100%)
    pallas_call x1, Pallas kernels, local(): pl.pallas_call(main_kernel, out_shape=[pltpu.VMEM((NF, 2, PAD, 128), f32)...  69.8 us
    pallas_call x1, Pallas kernels, local(): pl.pallas_call(final_kernel, out_shape=jax.ShapeDtypeStruct((9, LEVELS, R...  2.37 us

profile of v3, /device:TPU:1, one launch (start us, length us, event | category | flops | bytes accessed | tf_op | source)
XLA Modules:
  0.0 72.2 jit_solution(12229388219438789669)
XLA Ops:
  0.0 69.8 %main.1 = (f32[72,2,80,128]{3,2,1,0:T(8,128)S(1)}, f32[72,2,80,128]{3,2,1,0:T(8,128)S(1)}, f32[2,72,128]{2,1,0:T(8,128)S(1)}) custom-call(bf16[64,64,256]{2,1,0:T(8,128)(2,1)} %bitcast.4, f32[8,64,256]{2,1,0:T(8,128)} %kappa_in.1, f32[64,256]{1,0:T(8,128)} %cond_lat_in.1, f32[64,256]{1,0:T(8,128)} %cond_lon_in.1, f32[8,8192]{1,0:T(8,128)} %inno_in.1, ...), custom_call_target="tpu_custom_call" | custom-call | tf_op jit(solution)/shard_map/main/pallas_call | solution.py:484
  69.8 2.4 %final.1 = f32[9,8,64,256]{3,2,1,0:T(8,128)} custom-call(f32[72,2,80,128]{3,2,1,0:T(8,128)S(1)} %get-tuple-element.8.v0, f32[72,2,80,128]{3,2,1,0:T(8,128)S(1)} %get-tuple-element.9.v2, f32[2,72,128]{2,1,0:T(8,128)S(1)} %get-tuple-element.10.scale), custom_call_target="tpu_custom_call" | custom-call | tf_op jit(solution)/shard_map/final/pallas_call | solution.py:509

commit v4 on v3

--- a/solution.py
+++ b/solution.py
@@ -271,16 +271,21 @@
     def device(d):
         return (d // LON, lax.rem(d, LON))
 
-    def to_all(make):
-        for d in group_of(0)[1:]:
-            make(d).start()
+    def to_all(make, far_first=False):
+        def near():
+            for d in group_of(0)[1:]:
+                make(d).start()
 
         def rest(g, _):
-            for d in group_of(g):
+            for d in group_of(DEV // 8 - g if far_first else g):
                 make(d).start()
             return 0
 
+        if not far_first:
+            near()
         lax.fori_loop(1, DEV // 8, rest, 0)
+        if far_first:
+            near()
 
     def station_copy(src, dst):
         return pltpu.make_async_remote_copy(
@@ -416,7 +421,7 @@
         row = row + pltpu.roll(lane_totals(sums, k, NP, NA), NA * k, 1)
     tot[me, 2:3, :] = row
 
-    to_all(total_copy)
+    to_all(total_copy, far_first=True)
     others = pltpu.make_async_remote_copy(
         src_ref=send.at[pl.ds(0, DEV - 1)], dst_ref=got.at[pl.ds(0, DEV - 1)], send_sem=a2a_s, recv_sem=tot_r,
         device_id=lon_peers[0], device_id_type=MESH,

time: 72.3 us -> 71.9 us (level)
  no operation moved by 1% of the time
where the time goes in v4:
time: 71.9 us; the launch traced here: 71.8 us
  Pallas kernels  71.7 us (100%)
    pallas_call x1, Pallas kernels, local(): pl.pallas_call(main_kernel, out_shape=[pltpu.VMEM((NF, 2, PAD, 128), f32)...  69.4 us
    pallas_call x1, Pallas kernels, local(): pl.pallas_call(final_kernel, out_shape=jax.ShapeDtypeStruct((9, LEVELS, R...  2.37 us

profile of v4, /device:TPU:1, one launch (start us, length us, event | category | flops | bytes accessed | tf_op | source)
XLA Modules:
  0.0 71.8 jit_solution(18123689208704298674)
XLA Ops:
  0.0 69.4 %main.1 = (f32[72,2,80,128]{3,2,1,0:T(8,128)S(1)}, f32[72,2,80,128]{3,2,1,0:T(8,128)S(1)}, f32[2,72,128]{2,1,0:T(8,128)S(1)}) custom-call(bf16[64,64,256]{2,1,0:T(8,128)(2,1)} %bitcast.4, f32[8,64,256]{2,1,0:T(8,128)} %kappa_in.1, f32[64,256]{1,0:T(8,128)} %cond_lat_in.1, f32[64,256]{1,0:T(8,128)} %cond_lon_in.1, f32[8,8192]{1,0:T(8,128)} %inno_in.1, ...), custom_call_target="tpu_custom_call" | custom-call | tf_op jit(solution)/shard_map/main/pallas_call | solution.py:489
  69.4 2.4 %final.1 = f32[9,8,64,256]{3,2,1,0:T(8,128)} custom-call(f32[72,2,80,128]{3,2,1,0:T(8,128)S(1)} %get-tuple-element.8.v0, f32[72,2,80,128]{3,2,1,0:T(8,128)S(1)} %get-tuple-element.9.v2, f32[2,72,128]{2,1,0:T(8,128)S(1)} %get-tuple-element.10.scale), custom_call_target="tpu_custom_call" | custom-call | tf_op jit(solution)/shard_map/final/pallas_call | solution.py:514
